TPU v7x, 32 devices: a whole 2x2x4 slice. The times are simulated.
32 devices in a mesh: lat: 8 (over z, x), rad: 4 (over y, core).
Axes of the slice: x: 2, y: 2, z: 4, core: 2. Of those that a mesh axis runs over, the one named last changes fastest.
Arguments:
- kernels: float32 [3, 256000], P(None, 'lat'), may hold values from -6 to 6
- cells: int32 [3, 2048], P(None, 'lat'), may hold values from 0 to 251, as said below
- tiles: int32 [2048, 1], P('lat'), may hold values from 0 to 7; in each aligned block of 256 rows (0 to 255, 256 to 511, ...) at most 64 rows name the same one
- width_class: int32 [8], P('lat'), may hold values from 0 to 3
Outputs:
- smoothed: float32 [3, 64, 128, 256], P(None, 'lat', 'rad')
Inputs may be any that keep to these rules, and one draw needn't show every extreme that they name: `tiles`: of the elements of one index of lat, at most 64 name the same tile, a bound that some block reaches of them. cells[0, e] <= 3, cells[1, e] <= 123 and cells[2, e] <= 251, so that each element's 5 x 5 x 5 block lies in its tile; each bound is reached.
All inputs are finite; a program needn't handle non-finite values.
Results may differ from a plain program's by a relative error of at most 0.000078.
Values sent between devices are 32-bit elements; how exact they have to be, the bound alone decides.
A program may use at most 192 MiB of HBM per device.

v0:
```python
import jax
import jax.numpy as jnp
from jax import lax
from jax.sharding import PartitionSpec as P

CX = 8
NY = 256
CZ = 32
NGLL = 125
HW = 4
HY = 8
HZ = 4


def padded_2(value, sides, width):
    for axis, dim in sides:
        size, length = (lax.axis_size(axis), value.shape[dim])
        up = [(i, (i + 1) % size) for i in range(size - 1)]
        down = [(j, i) for i, j in up]
        last = lax.slice_in_dim(value, length - width, length, axis=dim)
        first = lax.slice_in_dim(value, 0, width, axis=dim)
        before = lax.ppermute(last, axis, up)
        after = lax.ppermute(first, axis, down)
        value = jnp.concatenate([before, value, after], axis=dim)
    return value


def band_weights(place, count, sigma, half):
    offsets = jnp.arange(-half, half + 1)
    target = place[:, None] + offsets[None, :]
    valid = (target >= 0) & (target < count)
    gauss = jnp.exp(-offsets[None, :].astype(jnp.float32) ** 2 / (2.0 * sigma[:, None] ** 2))
    gauss = jnp.where(valid, gauss, jnp.float32(0.0))
    return gauss / jnp.sum(gauss, axis=1, keepdims=True)


def point_cells(cells, depth):
    points = jnp.arange(NGLL, dtype=jnp.int32)
    along_x = points // 25
    along_z = points // 5 % 5
    along_y = points % 5
    return (
        (cells[0][:, None] + along_x[None, :]) * (depth * NY)
        + (cells[1][:, None] + along_z[None, :]) * NY
        + (cells[2][:, None] + along_y[None, :])
    )


def on_device(kernels, cells, tiles, width_class):
    n_lat = lax.axis_size("lat")
    n_rad = lax.axis_size("rad")
    elements = tiles.shape[0]
    capacity = max(2, 2 * elements // n_lat)
    depth = CZ * n_rad
    rows_total = CX * n_lat
    onehot = (tiles == jnp.arange(n_lat)[None, :]).astype(jnp.int32)
    ranks = jnp.cumsum(onehot, axis=0) - onehot
    slot_rank = jnp.sum(ranks * onehot, axis=1)
    slot_index = tiles[:, 0] * capacity + slot_rank
    send_vals = (
        jnp.zeros((3, n_lat * capacity, NGLL), jnp.float32)
        .at[:, slot_index]
        .set(kernels.reshape(3, elements, NGLL))
    )
    recv_vals = lax.all_to_all(
        send_vals.reshape(3, n_lat, capacity * NGLL), "lat", split_axis=1, concat_axis=1, tiled=True
    )
    recv_vals = recv_vals.reshape(3, -1)
    flat_cells = point_cells(cells, depth)
    send_cells = jnp.full((n_lat * capacity, NGLL), -1, jnp.int32).at[slot_index].set(flat_cells)
    recv_cells = lax.all_to_all(
        send_cells.reshape(n_lat, capacity * NGLL), "lat", split_axis=0, concat_axis=0, tiled=True
    )
    recv_cells = recv_cells.reshape(-1)
    slab = lax.axis_index("rad")
    cell_x = recv_cells // (depth * NY)
    cell_z = recv_cells // NY % depth - slab * CZ
    cell_y = recv_cells % NY
    inside = (recv_cells >= 0) & (cell_z >= 0) & (cell_z < CZ)
    local_cell = jnp.where(inside, (cell_x * CZ + cell_z) * NY + cell_y, CX * CZ * NY)
    summed = jnp.zeros((3, CX * CZ * NY), jnp.float32).at[:, local_cell].add(recv_vals, mode="drop")
    summed = summed.reshape(3, CX, CZ, NY)
    tile_index = lax.axis_index("lat")
    rows_here = tile_index * CX + jnp.arange(CX)
    sigma_x = jnp.full((CX,), 1.0, jnp.float32) + 0.75 * width_class[0].astype(jnp.float32)
    weights_x = band_weights(rows_here, rows_total, sigma_x, HW)
    padded = padded_2(summed, (("lat", 1),), HW)
    lateral = jnp.zeros_like(summed)
    for offset in range(-HW, HW + 1):
        lateral = (
            lateral
            + weights_x[:, offset + HW][None, :, None, None]
            * padded[:, HW + offset : HW + offset + CX]
        )
    every_y = jnp.arange(NY)
    weights_y = band_weights(every_y, NY, jnp.full((NY,), 2.5, jnp.float32), HY)
    gaps_y = every_y[None, :] - every_y[:, None]
    matrix_y = jnp.zeros((NY, NY), jnp.float32)
    for offset in range(-HY, HY + 1):
        matrix_y = matrix_y + jnp.where(
            gaps_y == offset, weights_y[:, offset + HY][:, None], jnp.float32(0.0)
        )
    across = jnp.einsum("cxzy,wy->cxzw", lateral, matrix_y, precision=lax.Precision.HIGHEST)
    planes_here = slab * CZ + jnp.arange(CZ)
    weights_z = band_weights(planes_here, depth, jnp.full((CZ,), 1.5, jnp.float32), HZ)
    padded_z = padded_2(across, (("rad", 2),), HZ)
    smoothed = jnp.zeros_like(across)
    for offset in range(-HZ, HZ + 1):
        smoothed = (
            smoothed
            + weights_z[:, offset + HZ][None, None, :, None]
            * padded_z[:, :, HZ + offset : HZ + offset + CZ]
        )
    return smoothed


def solution(mesh):
    return jax.shard_map(
        on_device,
        mesh=mesh,
        in_specs=(P(None, "lat"), P(None, "lat"), P("lat", None), P("lat")),
        out_specs=P(None, "lat", "rad", None),
        check_vma=False,
    )
```

profile of v0, /device:TPU:6, one launch (start us, length us, event | category | flops | bytes accessed | tf_op | source)
XLA Modules:
  0.0 476.4 jit_solution(710803126705207065)
XLA Ops:
  0.0 0.7 fusion.196
  0.7 0.6 reduce-window.6
  1.3 0.2 slice_reduce_fusion
  1.5 0.8 fusion.195
  2.3 0.7 compare_select_fusion.3
  3.0 0.8 fusion.222
  3.8 1.4 scatter_custom_fusion
  5.2 1.2 all_to_all.9
  6.4 6.3 %all-to-all-start = ((s32[8,1,8000]{2,1,0:T(1,128)}), s32[8,1,8000]{2,1,0:T(1,128)S(1)}, u32[]{:S(2)}, u32[]{:S(2)}) async-start(s32[8,1,8000]{2,1,0:T(1,128)} %all_to_all.9), calls=%async_computation | async-start | bytes 516096 | tf_op jit(solution)/shard_map/all_to_all | solution.py:71
  12.8 1.8 reshape.360
  14.6 0.3 copy.39
  15.0 7.0 %scatter_fusion = f32[3,512,125]{2,0,1:T(4,128)S(1)} fusion(f32[3,512,125]{2,0,1:T(4,128)S(1)} %broadcast_in_dim.194, s32[256]{0:T(256)S(1)} %bitcast.89, f32[256,3,125]{2,1,0:T(4,128)S(1)} %bitcast.81), kind=kCustom, calls=%fused_computation.1 | custom fusion | bytes 1153024 | tf_op jit(solution)/shard_map/scatter | solution.py:63
  22.1 0.5 reshape.346
  22.5 1.3 copy.29
  24.8 6.0 %all-to-all-start.1 = ((f32[3,8,8000]{2,0,1:T(4,128)}), f32[3,8,8000]{2,0,1:T(4,128)S(1)}, u32[]{:S(2)}, u32[]{:S(2)}) async-start(f32[3,8,8000]{2,0,1:T(4,128)} %copy.29), calls=%async_computation.1 | async-start | bytes 2064384 | tf_op jit(solution)/shard_map/all_to_all | solution.py:65
  31.0 0.6 reduce.1
  31.6 0.3 reshape.344
  31.9 4.7 fusion.136
  36.7 18.4 %all-to-all-done.1 = f32[3,8,8000]{2,0,1:T(4,128)S(1)} async-done(((f32[3,8,8000]{2,0,1:T(4,128)}), f32[3,8,8000]{2,0,1:T(4,128)S(1)}, u32[]{:S(2)}, u32[]{:S(2)}) %all-to-all-start.1) | async-done | bytes 768032 | tf_op jit(solution)/shard_map/all_to_all | solution.py:65
  55.1 0.6 reshape.368
  55.7 15.7 %copy.31 = f32[64000,3]{1,0:T(8,128)} copy(f32[64000,3]{0,1:T(4,128)S(1)} %bitcast.80) | data formatting | bytes 1536000 | tf_op jit(solution)/shard_map/reshape | solution.py:68
  71.4 352.5 %scatter_custom_fusion.2 = f32[3,65536]{0,1:T(8,128)} fusion(s32[64000]{0:T(1024)S(1)} %fusion.136, f32[64000,3]{1,0:T(8,128)} %copy.31, f32[]{:T(128)} %constant.133.clone.1), kind=kCustom, calls=%fused_computation.3 | custom fusion | flops 192000 | bytes 786944 | tf_op jit(solution)/shard_map/scatter-add | solution.py:81
  423.9 19.5 %copy.32 = f32[3,8,32,256]{3,2,1,0:T(8,128)S(1)} copy(f32[3,8,32,256]{0,3,2,1:T(8,128)} %bitcast.79) | data formatting | bytes 1572864 | tf_op jit(solution)/shard_map/reshape | solution.py:82
  443.4 2.7 collective-permute-start.1
  446.2 4.2 collective-permute-start
  450.5 5.9 %collective-permute-done.1 = f32[3,4,32,256]{3,2,1,0:T(8,128)S(1)} collective-permute-done((f32[3,4,32,256]{3,2,1,0:T(8,128)S(1)}, f32[3,4,32,256]{3,2,1,0:T(8,128)S(1)}, u32[]{:S(2)}, u32[]{:S(2)}) %collective-permute-start.1) | collective-permute-done | bytes 393248 | tf_op jit(solution)/shard_map/ppermute | solution.py:23
  456.4 8.3 %collective-permute-done = f32[3,4,32,256]{3,2,1,0:T(8,128)S(1)} collective-permute-done((f32[3,4,32,256]{3,2,1,0:T(8,128)S(1)}, f32[3,4,32,256]{3,2,1,0:T(8,128)S(1)}, u32[]{:S(2)}, u32[]{:S(2)}) %collective-permute-start) | collective-permute-done | bytes 393248 | tf_op jit(solution)/shard_map/ppermute | solution.py:22
  464.7 1.8 fusion.26
  466.5 2.0 collective-permute-start.3
  468.6 2.3 collective-permute-start.2
  470.9 3.6 collective-permute-done.2
  474.5 1.9 fusion.5
  (27 shorter events, 1.0 us)
Async XLA Ops:
  6.4 18.4 %all-to-all-start = ((s32[8,1,8000]{2,1,0:T(1,128)}), s32[8,1,8000]{2,1,0:T(1,128)S(1)}, u32[]{:S(2)}, u32[]{:S(2)}) async-start(s32[8,1,8000]{2,1,0:T(1,128)} %all_to_all.9), calls=%async_computation | async-start | bytes 516096 | tf_op jit(solution)/shard_map/all_to_all | solution.py:71
  24.8 30.3 %all-to-all-start.1 = ((f32[3,8,8000]{2,0,1:T(4,128)}), f32[3,8,8000]{2,0,1:T(4,128)S(1)}, u32[]{:S(2)}, u32[]{:S(2)}) async-start(f32[3,8,8000]{2,0,1:T(4,128)} %copy.29), calls=%async_computation.1 | async-start | bytes 2064384 | tf_op jit(solution)/shard_map/all_to_all | solution.py:65
  443.4 13.0 %collective-permute-start.1 = (f32[3,4,32,256]{3,2,1,0:T(8,128)S(1)}, f32[3,4,32,256]{3,2,1,0:T(8,128)S(1)}, u32[]{:S(2)}, u32[]{:S(2)}) collective-permute-start(f32[3,4,32,256]{3,2,1,0:T(8,128)S(1)} %get-tuple-element.8), channel_id=1, source_target_pairs={{4,0},{8,4},{12,8},{16,12},{20,16},{24,20},{28,24},{5,1},{9,5},{13... | collective-permute-start | bytes 1179656 | tf_op jit(solution)/shard_map/ppermute | solution.py:23
  446.2 18.5 %collective-permute-start = (f32[3,4,32,256]{3,2,1,0:T(8,128)S(1)}, f32[3,4,32,256]{3,2,1,0:T(8,128)S(1)}, u32[]{:S(2)}, u32[]{:S(2)}) collective-permute-start(f32[3,4,32,256]{3,2,1,0:T(8,128)S(1)} %get-tuple-element.7), channel_id=1, source_target_pairs={{0,4},{4,8},{8,12},{12,16},{16,20},{20,24},{24,28},{1,5},{5,9},{9,... | collective-permute-start | bytes 1179656 | tf_op jit(solution)/shard_map/ppermute | solution.py:22
  466.5 4.4 collective-permute-start.3
  468.6 5.9 %collective-permute-start.2 = (f32[3,8,4,256]{3,2,1,0:T(4,128)S(1)}, f32[3,8,4,256]{3,2,1,0:T(4,128)S(1)}, u32[]{:S(2)}, u32[]{:S(2)}) collective-permute-start(f32[3,8,4,256]{3,2,1,0:T(4,128)S(1)} %get-tuple-element.5), channel_id=1, source_target_pairs={{0,1},{1,2},{2,3},{4,5},{5,6},{6,7},{8,9},{9,10},{10,11},{12,13},{... | collective-permute-start | bytes 294920 | tf_op jit(solution)/shard_map/ppermute | solution.py:22
where the time goes:
time: 477 us; the launch traced here: 476 us
  other arithmetic  364 us (76%)
  local copies, waits for them, and re-layouts  49.4 us (10%)
  waiting for transfers between devices  36.3 us (8%)
  starting transfers between devices  23.6 us (5%)
    scatter-add x1, other arithmetic, on_device(): jnp.zeros((3, CX * CZ * NY), jnp.float32).at[:, local_cell]  353 us
    reshape x1, local copies, waits for them, and re-layouts, on_device(): summed = summed.reshape(3, CX, CZ, NY)  19.5 us
    all_to_all x1, waiting for transfers between devices, on_device(): lax.all_to_all(send_vals.reshape(3, n_lat, capacity * NGLL), 'lat', split...  18.4 us
    reshape x2, local copies, waits for them, and re-layouts, on_device(): recv_vals = recv_vals.reshape(3, -1)  16.3 us
    ppermute x2, waiting for transfers between devices, padded_2(): before = lax.ppermute(last, axis, up)  11.9 us
  transfers between devices with their start and end apart: 6, of which 4 were waited for; matrix products, arithmetic and copies ran while one was open for 4% of the time, Pallas kernels for 0%

commit v1 on v0

--- a/solution.py
+++ b/solution.py
@@ -62,8 +62,18 @@
         .at[:, slot_index]
         .set(kernels.reshape(3, elements, NGLL))
     )
-    recv_vals = lax.all_to_all(
-        send_vals.reshape(3, n_lat, capacity * NGLL), "lat", split_axis=1, concat_axis=1, tiled=True
+    recv_vals = jnp.concatenate(
+        lax.all_to_all(
+            jnp.stack(
+                jnp.split(
+                    send_vals.reshape(3, n_lat, capacity * NGLL), lax.axis_size("lat"), axis=1
+                )
+            ),
+            "lat",
+            0,
+            0,
+        ),
+        axis=1,
     )
     recv_vals = recv_vals.reshape(3, -1)
     flat_cells = point_cells(cells, depth)

time: 477 us -> 477 us (level)
  waiting for transfers between devices: 36.3 us -> 29.3 us
    another operation x1 -> x4, local copies, waits for them, and re-layouts: 0.01 us -> 17 us  [the longest x2 16.3 us: on_device(): recv_vals = recv_vals.reshape(3, -1)]
    reshape x2 -> x1, local copies, waits for them, and re-layouts: 16.3 us -> 0.05 us  [on_device(): jnp.concatenate(lax.all_to_all(jnp.stack(jnp.split(send_vals.reshape(3, n...]
    all_to_all x1, waiting for transfers between devices: 18.4 us -> 12.9 us  [on_device(): lax.all_to_all(jnp.stack(jnp.split(send_vals.reshape(3, n_lat, capacity *...]
    unnamed x0 -> x7, local copies, waits for them, and re-layouts: none -> 5.03 us
  transfers between devices with their start and end apart: 6 -> 6, of which waited for: 4 -> 4; matrix products, arithmetic and copies ran while one was open for 4% -> 5% of each run, Pallas kernels for 0% -> 0%
where the time goes in v1:
time: 477 us; the launch traced here: 474 us
  other arithmetic  364 us (76%)
  local copies, waits for them, and re-layouts  53.9 us (11%)
  waiting for transfers between devices  29.3 us (6%)
  starting transfers between devices  24 us (5%)
    scatter-add x1, other arithmetic, on_device(): jnp.zeros((3, CX * CZ * NY), jnp.float32).at[:, local_cell]  353 us
    reshape x1, local copies, waits for them, and re-layouts, on_device(): summed = summed.reshape(3, CX, CZ, NY)  19.5 us
    another operation x2, local copies, waits for them, and re-layouts, on_device(): recv_vals = recv_vals.reshape(3, -1)  16.3 us
    ppermute x2, waiting for transfers between devices, padded_2(): before = lax.ppermute(last, axis, up)  14.6 us
    all_to_all x1, waiting for transfers between devices, on_device(): lax.all_to_all(jnp.stack(jnp.split(send_vals.reshape(3, n_lat, capacity *...  12.9 us
  transfers between devices with their start and end apart: 6, of which 4 were waited for; matrix products, arithmetic and copies ran while one was open for 5% of the time, Pallas kernels for 0%

profile of v1, /device:TPU:6, one launch (start us, length us, event | category | flops | bytes accessed | tf_op | source)
XLA Modules:
  0.0 474.3 jit_solution(15463374406769371708)
XLA Ops:
  0.0 0.7 fusion.204
  1.5 0.8 fusion.203
  2.3 0.7 compare_select_fusion.3
  3.0 0.8 fusion.230
  3.8 1.4 scatter_custom_fusion
  5.2 1.2 all_to_all.9
  6.4 6.3 %all-to-all-start = ((s32[8,1,8000]{2,1,0:T(1,128)}), s32[8,1,8000]{2,1,0:T(1,128)S(1)}, u32[]{:S(2)}, u32[]{:S(2)}) async-start(s32[8,1,8000]{2,1,0:T(1,128)} %all_to_all.9), calls=%async_computation | async-start | bytes 516096 | tf_op jit(solution)/shard_map/all_to_all | solution.py:81
  12.8 1.8 reshape.360
  15.0 7.0 %scatter_fusion = f32[3,512,125]{2,0,1:T(4,128)S(1)} fusion(f32[3,512,125]{2,0,1:T(4,128)S(1)} %broadcast_in_dim.194, s32[256]{0:T(256)S(1)} %bitcast.127, f32[256,3,125]{2,1,0:T(4,128)S(1)} %bitcast.119), kind=kCustom, calls=%fused_computation.1 | custom fusion | bytes 1153024 | tf_op jit(solution)/shard_map/scatter | solution.py:63
  22.5 0.7 fusion.190
  23.2 0.7 fusion.189
  23.9 0.7 fusion.188
  24.7 0.7 fusion.187
  25.4 0.7 fusion.186
  26.1 0.7 fusion.185
  26.8 0.7 fusion.184
  27.6 0.7 fusion.183
  29.3 6.0 %all-to-all-start.1 = ((f32[8,3,1,8000]{3,2,1,0:T(1,128)}), f32[8,3,1,8000]{3,2,1,0:T(1,128)S(1)}, u32[]{:S(2)}, u32[]{:S(2)}) async-start(f32[8,3,1,8000]{3,2,1,0:T(1,128)} %fusion.183), calls=%async_computation.1 | async-start | bytes 1548288 | tf_op jit(solution)/shard_map/all_to_all | solution.py:66
  35.5 0.6 reduce.1
  36.4 4.7 %fusion.136 = s32[64000]{0:T(1024)S(1)} fusion(s32[64000,1]{0,1:T(1,128)S(1)} %reshape.344, s32[]{:T(128)S(6)} %mul.236), kind=kLoop, calls=%fused_computation.157 | loop fusion | flops 3456000 | bytes 512004 | tf_op jit(solution)/shard_map/select_n | solution.py:91
  41.1 12.9 %all-to-all-done.1 = f32[8,3,1,8000]{3,2,1,0:T(1,128)S(1)} async-done(((f32[8,3,1,8000]{3,2,1,0:T(1,128)}), f32[8,3,1,8000]{3,2,1,0:T(1,128)S(1)}, u32[]{:S(2)}, u32[]{:S(2)}) %all-to-all-start.1) | async-done | bytes 768032 | tf_op jit(solution)/shard_map/all_to_all | solution.py:66
  54.7 15.7 %copy.37 = f32[64000,3]{1,0:T(8,128)} copy(f32[64000,3]{0,1:T(4,128)S(1)} %bitcast.117) | data formatting | bytes 1536000 | tf_op jit(solution)/shard_map/reshape;reshape | solution.py:78
  70.3 352.5 %scatter_custom_fusion.2 = f32[3,65536]{0,1:T(8,128)} fusion(s32[64000]{0:T(1024)S(1)} %fusion.136, f32[64000,3]{1,0:T(8,128)} %copy.37, f32[]{:T(128)} %constant.133.clone.1), kind=kCustom, calls=%fused_computation.3 | custom fusion | flops 192000 | bytes 786944 | tf_op jit(solution)/shard_map/scatter-add | solution.py:91
  422.9 19.5 %copy.38 = f32[3,8,32,256]{3,2,1,0:T(8,128)S(1)} copy(f32[3,8,32,256]{0,3,2,1:T(8,128)} %bitcast.116) | data formatting | bytes 1572864 | tf_op jit(solution)/shard_map/reshape | solution.py:92
  442.4 2.3 collective-permute-start
  444.7 3.7 collective-permute-start.1
  448.5 14.2 %collective-permute-done = f32[3,4,32,256]{3,2,1,0:T(8,128)S(1)} collective-permute-done((f32[3,4,32,256]{3,2,1,0:T(8,128)S(1)}, f32[3,4,32,256]{3,2,1,0:T(8,128)S(1)}, u32[]{:S(2)}, u32[]{:S(2)}) %collective-permute-start) | collective-permute-done | bytes 393248 | tf_op jit(solution)/shard_map/ppermute | solution.py:22
  462.8 1.8 fusion.26
  464.6 1.9 collective-permute-start.2
  466.5 3.6 collective-permute-start.3
  470.5 1.8 collective-permute-done.3
  472.4 1.9 fusion.5
  (34 shorter events, 3.7 us)
Async XLA Ops:
  6.4 22.9 %all-to-all-start = ((s32[8,1,8000]{2,1,0:T(1,128)}), s32[8,1,8000]{2,1,0:T(1,128)S(1)}, u32[]{:S(2)}, u32[]{:S(2)}) async-start(s32[8,1,8000]{2,1,0:T(1,128)} %all_to_all.9), calls=%async_computation | async-start | bytes 516096 | tf_op jit(solution)/shard_map/all_to_all | solution.py:81
  29.3 24.7 %all-to-all-start.1 = ((f32[8,3,1,8000]{3,2,1,0:T(1,128)}), f32[8,3,1,8000]{3,2,1,0:T(1,128)S(1)}, u32[]{:S(2)}, u32[]{:S(2)}) async-start(f32[8,3,1,8000]{3,2,1,0:T(1,128)} %fusion.183), calls=%async_computation.1 | async-start | bytes 1548288 | tf_op jit(solution)/shard_map/all_to_all | solution.py:66
  442.4 20.4 %collective-permute-start = (f32[3,4,32,256]{3,2,1,0:T(8,128)S(1)}, f32[3,4,32,256]{3,2,1,0:T(8,128)S(1)}, u32[]{:S(2)}, u32[]{:S(2)}) collective-permute-start(f32[3,4,32,256]{3,2,1,0:T(8,128)S(1)} %get-tuple-element.7), channel_id=1, source_target_pairs={{0,4},{4,8},{8,12},{12,16},{16,20},{20,24},{24,28},{1,5},{5,9},{9,... | collective-permute-start | bytes 1179656 | tf_op jit(solution)/shard_map/ppermute | solution.py:22
  444.7 18.0 %collective-permute-start.1 = (f32[3,4,32,256]{3,2,1,0:T(8,128)S(1)}, f32[3,4,32,256]{3,2,1,0:T(8,128)S(1)}, u32[]{:S(2)}, u32[]{:S(2)}) collective-permute-start(f32[3,4,32,256]{3,2,1,0:T(8,128)S(1)} %get-tuple-element.8), channel_id=1, source_target_pairs={{4,0},{8,4},{12,8},{16,12},{20,16},{24,20},{28,24},{5,1},{9,5},{13... | collective-permute-start | bytes 1179656 | tf_op jit(solution)/shard_map/ppermute | solution.py:23
  464.6 5.9 %collective-permute-start.2 = (f32[3,8,4,256]{3,2,1,0:T(4,128)S(1)}, f32[3,8,4,256]{3,2,1,0:T(4,128)S(1)}, u32[]{:S(2)}, u32[]{:S(2)}) collective-permute-start(f32[3,8,4,256]{3,2,1,0:T(4,128)S(1)} %get-tuple-element.5), channel_id=1, source_target_pairs={{0,1},{1,2},{2,3},{4,5},{5,6},{6,7},{8,9},{9,10},{10,11},{12,13},{... | collective-permute-start | bytes 294920 | tf_op jit(solution)/shard_map/ppermute | solution.py:22
  466.5 5.8 %collective-permute-start.3 = (f32[3,8,4,256]{3,2,1,0:T(4,128)S(1)}, f32[3,8,4,256]{3,2,1,0:T(4,128)S(1)}, u32[]{:S(2)}, u32[]{:S(2)}) collective-permute-start(f32[3,8,4,256]{3,2,1,0:T(4,128)S(1)} %get-tuple-element.6), channel_id=1, source_target_pairs={{1,0},{2,1},{3,2},{5,4},{6,5},{7,6},{9,8},{10,9},{11,10},{13,12},{... | collective-permute-start | bytes 294920 | tf_op jit(solution)/shard_map/ppermute | solution.py:23
